TPU v7x, 512 devices: a whole 4x4x16 slice. The times are simulated.
512 devices in a mesh: blk: 128 (over x, z_lo, y), probe: 4 (over z_hi, core).
Axes of the slice: x: 4, y: 4, z: 16 (z_hi: 2, z_lo: 8; z = z_hi * 8 + z_lo), core: 2. Of those that a mesh axis runs over, the one named last changes fastest.
Arguments:
- positions: bfloat16 [3, 4096], P(None, 'blk'), may hold values from 0 to 4
- scales: bfloat16 [4096], P('blk'), may hold values from 0.5 to 2
- onsite: float32 [4096], P('blk'), may hold values from 0.5 to 1.5
- probes: bfloat16 [3, 64, 4096], P(None, 'probe', 'blk'), may hold values from -4 to 4
Outputs:
- chebyshev_two: float32 [3, 64, 4096], P(None, 'probe', 'blk')
- forces: float32 [3, 4096], P(None, 'blk')
- energy: float32 [], replicated
All inputs are finite; a program needn't handle non-finite values.
Results may differ from a plain program's by a relative error of at most 0.0015.
Values may be sent and summed in bfloat16 or wider, within the bound.
No kernel may reach another device: no remote copies, remote signals or barrier semaphores. Data moves between devices by JAX's collectives and lax.ppermute only.
A program may use at most 64 MiB of HBM per device.

v0:
```python
import math

import jax
import jax.numpy as jnp
from jax import lax
from jax.experimental import pallas as pl
from jax.experimental.pallas import tpu as pltpu
from jax.sharding import Mesh, PartitionSpec as P

SOFT_SQ = 0.25
F32 = jnp.float32
BF16 = jnp.bfloat16

NX, NZL, NY, NZH, NC = 4, 8, 4, 2, 2
PLANE = NX * NY
LINE = NZL * NZH
A = 32
NP = 16
CH = NZL * A
PR = NZH * NP
VEC = 3 * PR
ROWS = 2 * VEC + 16
HALF = CH // 2
VMEM = 48 * 1024 * 1024


def split3(value):
    hi = value.astype(BF16)
    rest = value - hi.astype(F32)
    mid = rest.astype(BF16)
    low = (rest - mid.astype(F32)).astype(BF16)
    return hi.astype(F32), mid.astype(F32), low.astype(F32)


def pack_kernel(pos_in, scale_in, onsite_in, probe_in, out_ref, pos_ref, scale_ref, onsite_ref, probe_ref, sems):
    pairs = ((pos_in, pos_ref), (scale_in, scale_ref), (onsite_in, onsite_ref), (probe_in, probe_ref))
    copies = [pltpu.make_async_copy(a, b, sems.at[k]) for k, (a, b) in enumerate(pairs)]
    for copy in copies:
        copy.start()
    for copy in copies:
        copy.wait()
    hi, mid, low = split3(onsite_ref[...])
    row = lax.broadcasted_iota(jnp.int32, (16, A), 0)
    meta = jnp.zeros((16, A), F32)
    pos = pos_ref[...].astype(F32)
    values = [pos[0:1], pos[1:2], pos[2:3], scale_ref[...].astype(F32), hi, mid, low]
    for k, value in enumerate(values):
        meta = jnp.where(row == k, jnp.broadcast_to(value, (16, A)), meta)
    parts = [probe_ref[c].astype(F32) for c in range(3)] + [meta]
    packet = jnp.concatenate(parts, axis=1).astype(BF16)
    for k in range(LINE):
        out_ref[k] = packet


def line_kernel(in_ref, out_ref):
    parts, values = [], []
    for first in (0, NZL // 2):
        lines = range(first, first + NZL // 2)
        for q in range(3):
            for zh in range(NZH):
                parts.append(jnp.concatenate(
                    [in_ref[zl * NZH + zh, :, q * A:(q + 1) * A] for zl in lines], axis=1))
        values.append(jnp.concatenate(
            [in_ref[zl * NZH, :, 3 * A:4 * A].astype(F32) for zl in lines], axis=1)[0:8])
    parts.append(jnp.concatenate(values, axis=0).astype(BF16))
    packet = jnp.concatenate(parts, axis=0)
    for k in range(PLANE):
        out_ref[k] = packet


def vectors_of(ref, k):
    return jnp.concatenate([ref[k, 0:VEC], ref[k, VEC:2 * VEC]], axis=1)


def values_of(ref, k):
    both = ref[k, 2 * VEC:ROWS].astype(F32)
    return jnp.concatenate([both[0:8], both[8:16]], axis=1)


def geometry(xi, yi, zi, si, xj, yj, zj, sj):
    rx, ry, rz = xi - xj, yi - yj, zi - zj
    q = lax.rsqrt(rx * rx + ry * ry + rz * rz + SOFT_SQ)
    q2 = q * q
    a = (si * sj) * (q2 * q)
    b = (3.0 * a) * q2
    return rx, ry, rz, q2, a, b


def tensor(rx, ry, rz, a, b):
    tx, ty, tz = rx * b, ry * b, rz * b
    return (tx * rx - a, tx * ry, tx * rz, ty * ry - a, ty * rz, tz * rz - a)


def doubled(xi, yi, zi, si, xj, yj, zj, sj):
    rx, ry, rz = xi - xj, yi - yj, zi - zj
    q = lax.rsqrt(rx * rx + ry * ry + rz * rz + 4.0 * SOFT_SQ)
    q2 = q * q
    a = (si * sj) * (q2 * q)
    b = (3.0 * a) * q2
    tx, ty = rx * b, ry * b
    xx, yy = tx * rx - a, ty * ry - a
    return (xx, tx * ry, tx * rz, yy, ty * rz, -b - (xx + yy))


NT = (((1,), (1,)), ((), ()))


def columns(vectors, values):
    rest = jnp.zeros((128 - VEC - values.shape[0], CH), F32)
    return jnp.concatenate([vectors.astype(F32), values, rest], axis=0).T


def step_kernel(ids, strength, far_ref, out_ref, even_ref, odd_ref, col_ref, acc_ref):
    own = ids()[0]
    values = values_of(far_ref, own)
    turned = columns(vectors_of(far_ref, own), values)
    for k in range(4):
        column = turned[:, VEC + k:VEC + k + 1]
        col_ref[k] = jnp.broadcast_to(column if k == 3 else 2.0 * column, (CH, 128))
    acc_ref[...] = jnp.zeros_like(acc_ref)
    sub = 16

    def build(jc, tile_ref):
        v = values_of(far_ref, jc)
        xj, yj, zj, sj = 2.0 * v[0:1], 2.0 * v[1:2], 2.0 * v[2:3], v[3:4] * (8.0 * strength)
        for i0 in range(0, CH, sub):
            rows = slice(i0, i0 + sub)
            near = [col_ref[k, rows] for k in range(4)]
            for half in range(2):
                lanes = slice(half * 128, half * 128 + 128)
                tile = doubled(*near, xj[:, lanes], yj[:, lanes], zj[:, lanes], sj[:, lanes])
                for k, value in enumerate(tile):
                    tile_ref[k, rows, lanes] = value.astype(BF16)

    def multiply(jc, tile_ref):
        vec = vectors_of(far_ref, jc)
        vx, vy, vz = vec[0:PR], vec[PR:2 * PR], vec[2 * PR:]

        def times(lhs, k):
            return lax.dot_general(lhs, tile_ref[k], NT, preferred_element_type=F32)

        xx, yy, zz = times(vx, 0), times(vy, 3), times(vz, 5)
        xy = times(vec[0:2 * PR], 1)
        yz = times(vec[PR:], 4)
        xz = times(jnp.concatenate([vx, vz], axis=0), 2)
        acc_ref[0:PR] += xx + xy[PR:] + xz[PR:]
        acc_ref[PR:2 * PR] += yy + xy[:PR] + yz[PR:]
        acc_ref[2 * PR:] += zz + xz[:PR] + yz[:PR]

    build(0, even_ref)

    def turn(jc, carry):
        @pl.when(lax.rem(jc, 2) == 0)
        def _():
            build(jc + 1, odd_ref)
            multiply(jc, even_ref)

        @pl.when((lax.rem(jc, 2) == 1) & (jc < PLANE - 1))
        def _():
            build(jc + 1, even_ref)
            multiply(jc, odd_ref)
        return carry

    lax.fori_loop(0, PLANE, turn, 0)
    multiply(PLANE - 1, odd_ref)
    onsite = values[4:5] + values[5:6] + values[6:7]
    z = vectors_of(far_ref, own).astype(F32)
    still = values[0:1] - values[0:1]
    pair = doubled(still, still, still, values[3:4], still, still, still, values[3:4] * (8.0 * strength))
    kept = [jnp.broadcast_to(pair[k].astype(BF16).astype(F32), (PR, CH)) for k in (0, 3, 5)]
    exact = onsite * z + (acc_ref[...] - jnp.concatenate(kept, axis=0) * z)
    step = exact.astype(BF16)
    w = step.astype(F32)
    part = 0.5 * (z - exact) * w + 0.25 * z * z
    total = jnp.sum(jnp.sum(part, axis=0, keepdims=True), axis=1, keepdims=True)
    pieces = split3(total)
    row = lax.broadcasted_iota(jnp.int32, (16, HALF), 0)
    extra = jnp.zeros((16, HALF), F32)
    for k in range(3):
        extra = jnp.where(row == k, jnp.broadcast_to(pieces[k], (16, HALF)), extra)
    result = jnp.concatenate([step[:, :HALF], step[:, HALF:], extra.astype(BF16)], axis=0)
    for k in range(PLANE):
        out_ref[k] = result


def transposed(value):
    return jnp.concatenate([value, jnp.zeros((128 - A, 128), F32)], axis=0).T


def final_kernel(ids, strength, far_ref, step_ref, onsite_ref, probe_ref, cheb_ref, side_ref, colz_ref, colw_ref):
    own, zl, zh = ids()
    colz_ref[...] = columns(vectors_of(far_ref, own), values_of(far_ref, own))
    colw_ref[...] = columns(vectors_of(step_ref, own), jnp.zeros((8, CH), F32))
    mine = pl.ds(pl.multiple_of(zl * A, A), A)
    zi, wi = colz_ref[mine], colw_ref[mine]
    near = [jnp.broadcast_to(zi[:, VEC + k:VEC + k + 1], (A, CH)) for k in range(4)]
    left = []
    for c in range(3):
        lanes = slice(c * PR, (c + 1) * PR)
        zc, wc = 0.5 * zi[:, lanes], -0.5 * wi[:, lanes]
        left.append(jnp.concatenate([zc, wc, -zc], axis=1))
    left = jnp.concatenate(left, axis=0).astype(BF16)
    row = lax.broadcasted_iota(jnp.int32, (A, CH), 0)
    lane = lax.broadcasted_iota(jnp.int32, (A, CH), 1)

    def chunk(jc, carry):
        gx, gy, gz, image, energy = carry
        meta = values_of(far_ref, jc)
        rx, ry, rz, q2, a, b = geometry(
            *near, meta[0:1], meta[1:2], meta[2:3], meta[3:4] * strength)
        same = row + (own * CH + zl * A) == lane + jc * CH
        xx, xy, xz, yy, yz, zz = tensor(rx, ry, rz, jnp.where(same, 0.0, a), b)
        z, w = vectors_of(far_ref, jc), vectors_of(step_ref, jc)
        kinds = ((xx, xy, xz), (xy, yy, yz), (xz, yz, zz))
        weight = []
        for d in range(3):
            rows = slice(d * PR, (d + 1) * PR)
            tile = jnp.concatenate(kinds[d], axis=0).astype(BF16)
            image = image + lax.dot_general(w[rows], tile, NT, preferred_element_type=F32)
            right = jnp.concatenate([z[rows], z[rows], w[rows]], axis=0)
            weight.append(jnp.dot(left, right, preferred_element_type=F32))

        def wt(c, d):
            return weight[d][c * A:(c + 1) * A]

        trace = wt(0, 0) + wt(1, 1) + wt(2, 2)
        sxy, sxz, syz = wt(0, 1) + wt(1, 0), wt(0, 2) + wt(2, 0), wt(1, 2) + wt(2, 1)
        ux = 2.0 * wt(0, 0) * rx + sxy * ry + sxz * rz
        uy = sxy * rx + 2.0 * wt(1, 1) * ry + syz * rz
        uz = sxz * rx + syz * ry + 2.0 * wt(2, 2) * rz
        radial = trace - 2.5 * q2 * (rx * ux + ry * uy + rz * uz)
        gx = gx + b * (ux + rx * radial)
        gy = gy + b * (uy + ry * radial)
        gz = gz + b * (uz + rz * radial)
        piece = step_ref[jc, 2 * VEC:ROWS].astype(F32)
        energy = energy + (piece[0:1] + piece[1:2] + piece[2:3])
        return gx, gy, gz, image, energy

    zero = jnp.zeros((A, CH), F32)
    gx, gy, gz, image, energy = lax.fori_loop(
        0, PLANE, chunk,
        (zero, zero, zero, jnp.zeros((PR, 3 * A), F32), jnp.zeros((1, HALF), F32)),
        unroll=16)
    w_rows = transposed(wi)
    for c in range(3):
        both = image[:, c * A:(c + 1) * A]
        w_both = w_rows[c * PR:(c + 1) * PR, 0:A]
        high = jnp.full((NP, A), zh, jnp.int32) > 0
        part = jnp.where(high, both[NP:], both[:NP])
        w = jnp.where(high, w_both[NP:], w_both[:NP])
        cheb_ref[c] = 2.0 * (onsite_ref[...] * w + part) - probe_ref[c].astype(F32)
    out = []
    for g in (gx, gy, gz):
        out.append(jnp.sum(transposed(g[:, 0:128] + g[:, 128:256]), axis=0, keepdims=True))
    out.append(energy)
    side = jnp.concatenate(out + [jnp.zeros((4, 128), F32)], axis=0)
    side_ref[...] = side


def spec():
    return pl.BlockSpec(memory_space=pltpu.VMEM)


def call(kernel, outs, scratch, operands):
    return pl.pallas_call(
        kernel,
        out_shape=outs,
        in_specs=[spec() for _ in operands],
        out_specs=jax.tree.map(lambda _: spec(), outs),
        scratch_shapes=scratch,
        compiler_params=pltpu.CompilerParams(vmem_limit_bytes=VMEM),
    )(*operands)


def pack(*operands):
    scratch = [pltpu.VMEM(x.shape, x.dtype) for x in operands] + [pltpu.SemaphoreType.DMA((4,))]
    return pl.pallas_call(
        pack_kernel,
        out_shape=jax.ShapeDtypeStruct((LINE, 16, 4 * A), BF16),
        in_specs=[pl.BlockSpec(memory_space=pltpu.HBM) for _ in operands],
        out_specs=spec(),
        scratch_shapes=scratch,
        compiler_params=pltpu.CompilerParams(vmem_limit_bytes=VMEM),
    )(*(pltpu.with_memory_space_constraint(x, pltpu.HBM) for x in operands))


def line(gathered):
    return call(line_kernel, jax.ShapeDtypeStruct((PLANE, ROWS, HALF), BF16), [], (gathered,))


def step(ids, strength, far):
    def kernel(*refs):
        step_kernel(ids, strength, *refs)
    scratch = [pltpu.VMEM((6, CH, CH), BF16), pltpu.VMEM((6, CH, CH), BF16), pltpu.VMEM((4, CH, 128), F32), pltpu.VMEM((VEC, CH), F32)]
    return call(kernel, jax.ShapeDtypeStruct((PLANE, ROWS, HALF), BF16), scratch, (far,))


def final(ids, strength, far, steps, onsite, probes):
    def kernel(*refs):
        final_kernel(ids, strength, *refs)
    outs = (jax.ShapeDtypeStruct((3, NP, A), F32), jax.ShapeDtypeStruct((8, 128), F32))
    scratch = [pltpu.VMEM((CH, 128), F32), pltpu.VMEM((CH, 128), F32)]
    return call(kernel, outs, scratch, (far, steps, onsite, probes))


def end_kernel(probe_total, side_ref, image_ref, cheb_ref, forces_ref, energy_ref):
    cheb_ref[...] = image_ref[...]
    both = side_ref[0:8] + side_ref[8:16]
    forces_ref[...] = (-2.0 / probe_total) * both[0:3, 0:A]
    energy_ref[...] = both[3:4, 0:1] / probe_total


def end(probe_total, sides, cheb):
    def kernel(*refs):
        end_kernel(probe_total, *refs)
    shapes = ((3, NP, A), (3, A), (1, 1))
    outs = tuple(jax.ShapeDtypeStruct(x, F32) for x in shapes)
    return call(kernel, outs, [], (sides, cheb))


def place():
    return (lax.axis_index("x") * NY + lax.axis_index("y"), lax.axis_index("zl"), lax.axis_index("zh"))


def body(positions, scales, onsite, probes):
    atoms = A * NX * NZL * NY
    probe_total = NP * NZH * NC
    strength = 4.0 / math.sqrt(atoms)
    scales, onsite = scales[None, :], onsite[None, :]
    sent = pack(positions, scales, onsite, probes)
    gathered = lax.all_to_all(sent, ("zl", "zh"), 0, 0, tiled=True)
    far = lax.all_to_all(line(gathered), ("x", "y"), 0, 0, tiled=True)
    steps = lax.all_to_all(step(place, strength, far), ("x", "y"), 0, 0, tiled=True)
    cheb, side = final(place, strength, far, steps, onsite, probes)
    sides = lax.all_gather(side, "c", axis=0, tiled=True)
    cheb, forces, energy = end(probe_total, sides, cheb)
    return cheb, forces, energy.reshape(())


def solution(mesh):
    fine = Mesh(mesh.devices.reshape(NX, NZL, NY, NZH, NC), ("x", "zl", "y", "zh", "c"))
    blk, probe = ("x", "zl", "y"), ("zh", "c")
    return jax.shard_map(
        body,
        mesh=fine,
        in_specs=(P(None, blk), P(blk), P(blk), P(None, probe, blk)),
        out_specs=(P(None, probe, blk), P(None, blk), P()),
        check_vma=False,
    )
```

profile of v0, /device:TPU:1, one launch (start us, length us, event | category | flops | bytes accessed | tf_op | source)
XLA Modules:
  0.0 78.2 jit_solution(17560259593148759757)
XLA Ops:
  0.6 0.9 %shard_map.67 = bf16[16,16,128]{2,1,0:T(8,128)(2,1)S(1)} custom-call(bf16[3,32]{1,0:T(4,128)(2,1)} %pos_in.1, bf16[1,32]{1,0:T(2,128)(2,1)} %bitcast.5, f32[1,32]{1,0:T(1,128)} %bitcast.3, bf16[3,16,32]{2,1,0:T(8,128)(2,1)} %refs_3_.1), custom_call_target="tpu_custom_call" | custom-call | tf_op jit(solution)/shard_map/pallas_call | solution.py:277
  1.5 27.7 %all_to_all.15.in_ref = bf16[16,16,128]{2,1,0:T(8,128)(2,1)S(1)} all-to-all(bf16[16,16,128]{2,1,0:T(8,128)(2,1)S(1)} %shard_map.67), channel_id=1, replica_groups=mesh['x'=4,'zl'=8,'y'=4,'zh'=2,'c'=2] {'zl','zh'}, dimensions={0} | all-to-all | bytes 131072 | tf_op jit(solution)/shard_map/all_to_all | solution.py:331
  29.2 0.2 shard_map.68
  29.4 18.9 %all_to_all.16.refs_0_ = bf16[16,208,128]{2,1,0:T(8,128)(2,1)S(1)} all-to-all(bf16[16,208,128]{2,1,0:T(8,128)(2,1)S(1)} %shard_map.68), channel_id=1, replica_groups=mesh['x'=4,'zl'=8,'y'=4,'zh'=2,'c'=2] {'x','y'}, dimensions={0} | all-to-all | bytes 1703936 | tf_op jit(solution)/shard_map/all_to_all | solution.py:332
  48.3 6.7 %shard_map.69 = bf16[16,208,128]{2,1,0:T(8,128)(2,1)S(1)} custom-call(bf16[16,208,128]{2,1,0:T(8,128)(2,1)S(1)} %all_to_all.16.refs_0_), custom_call_target="tpu_custom_call" | custom-call | tf_op jit(solution)/shard_map/pallas_call | solution.py:265
  55.0 0.0 copy-start
  55.0 0.0 copy-start.1
  55.0 14.0 %all_to_all.17.refs_1_ = bf16[16,208,128]{2,1,0:T(8,128)(2,1)S(1)} all-to-all(bf16[16,208,128]{2,1,0:T(8,128)(2,1)S(1)} %shard_map.69), channel_id=1, replica_groups=mesh['x'=4,'zl'=8,'y'=4,'zh'=2,'c'=2] {'x','y'}, dimensions={0} | all-to-all | bytes 1703936 | tf_op jit(solution)/shard_map/all_to_all | solution.py:333
  69.0 0.0 copy-done
  69.0 0.0 copy-done.1
  69.0 1.9 %shard_map.70 = (f32[3,16,32]{2,1,0:T(8,128)S(1)}, f32[8,128]{1,0:T(8,128)S(1)}) custom-call(bf16[16,208,128]{2,1,0:T(8,128)(2,1)S(1)} %all_to_all.16.refs_0_, bf16[16,208,128]{2,1,0:T(8,128)(2,1)S(1)} %all_to_all.17.refs_1_, f32[1,32]{1,0:T(1,128)S(1)} %bitcast.4, bf16[3,16,32]{2,1,0:T(8,128)(2,1)S(1)} %copy-done), custom_call_target="tpu_custom_call" | custom-call | tf_op jit(solution)/shard_map/pallas_call | solution.py:265
  70.9 6.6 %all_gather.3.refs_0_ = f32[16,128]{1,0:T(8,128)S(1)} all-gather(f32[8,128]{1,0:T(8,128)S(1)} %get-tuple-element.8), channel_id=1, replica_groups=mesh['x'=4,'zl'=8,'y'=4,'zh'=2,'c'=2] {'c'}, dimensions={0}, use_global_device_ids=true | all-gather | bytes 12288 | tf_op jit(solution)/shard_map/all_gather | solution.py:335
  77.6 0.6 shard_map.71
Async XLA Ops:
  55.0 14.0 %copy-start = (bf16[3,16,32]{2,1,0:T(8,128)(2,1)S(1)}, bf16[3,16,32]{2,1,0:T(8,128)(2,1)}, u32[]{:S(2)}) copy-start(bf16[3,16,32]{2,1,0:T(8,128)(2,1)} %refs_3_.1) | copy-start | bytes 9220
  55.0 14.0 %copy-start.1 = (f32[32]{0:T(128)S(1)}, f32[32]{0:T(128)}, u32[]{:S(2)}) copy-start(f32[32]{0:T(128)} %param.6) | copy-start | bytes 388
where the time goes:
time: 78.5 us; the launch traced here: 78.2 us
  blocking collectives  67.2 us (86%)
  Pallas kernels  10.3 us (13%)
    all_to_all x1, blocking collectives, body(): gathered = lax.all_to_all(sent, ('zl', 'zh'), 0, 0, tiled=True)  27.7 us
    all_to_all x1, blocking collectives, body(): far = lax.all_to_all(line(gathered), ('x', 'y'), 0, 0, tiled=True)  18.9 us
    all_to_all x1, blocking collectives, body(): lax.all_to_all(step(place, strength, far), ('x', 'y'), 0, 0, tiled=True)  14 us
    pallas_call x4, Pallas kernels, call(): pl.pallas_call(kernel, out_shape=outs, in_specs=[spec() for _ in operands...  9.46 us
    all_gather x1, blocking collectives, body(): sides = lax.all_gather(side, 'c', axis=0, tiled=True)  6.65 us

commit v1 on v0

--- a/solution.py
+++ b/solution.py
@@ -32,13 +32,7 @@
     return hi.astype(F32), mid.astype(F32), low.astype(F32)
 
 
-def pack_kernel(pos_in, scale_in, onsite_in, probe_in, out_ref, pos_ref, scale_ref, onsite_ref, probe_ref, sems):
-    pairs = ((pos_in, pos_ref), (scale_in, scale_ref), (onsite_in, onsite_ref), (probe_in, probe_ref))
-    copies = [pltpu.make_async_copy(a, b, sems.at[k]) for k, (a, b) in enumerate(pairs)]
-    for copy in copies:
-        copy.start()
-    for copy in copies:
-        copy.wait()
+def pack_kernel(pos_ref, scale_ref, onsite_ref, probe_ref, out_ref):
     hi, mid, low = split3(onsite_ref[...])
     row = lax.broadcasted_iota(jnp.int32, (16, A), 0)
     meta = jnp.zeros((16, A), F32)
@@ -273,15 +267,7 @@
 
 
 def pack(*operands):
-    scratch = [pltpu.VMEM(x.shape, x.dtype) for x in operands] + [pltpu.SemaphoreType.DMA((4,))]
-    return pl.pallas_call(
-        pack_kernel,
-        out_shape=jax.ShapeDtypeStruct((LINE, 16, 4 * A), BF16),
-        in_specs=[pl.BlockSpec(memory_space=pltpu.HBM) for _ in operands],
-        out_specs=spec(),
-        scratch_shapes=scratch,
-        compiler_params=pltpu.CompilerParams(vmem_limit_bytes=VMEM),
-    )(*(pltpu.with_memory_space_constraint(x, pltpu.HBM) for x in operands))
+    return call(pack_kernel, jax.ShapeDtypeStruct((LINE, 16, 4 * A), BF16), [], operands)
 
 
 def line(gathered):

time: 78.5 us -> 79 us (level)
  local copies, waits for them, and re-layouts: 0.01 us -> 1.4 us
    unnamed x4 -> x10, local copies, waits for them, and re-layouts: 0.01 us -> 1.4 us
    pallas_call x1 -> x0, Pallas kernels: 0.88 us -> none  [pack(): pl.pallas_call(pack_kernel, out_shape=jax.ShapeDtypeStruct((LINE, 16, 4 *...]
    pallas_call x4 -> x5, Pallas kernels: 9.46 us -> 9.56 us  [call(): pl.pallas_call(kernel, out_shape=outs, in_specs=[spec() for _ in operands...]
where the time goes in v1:
time: 79 us; the launch traced here: 78.7 us
  blocking collectives  67 us (85%)
  Pallas kernels  9.56 us (12%)
  local copies, waits for them, and re-layouts  1.4 us (2%)
    all_to_all x1, blocking collectives, body(): gathered = lax.all_to_all(sent, ('zl', 'zh'), 0, 0, tiled=True)  27.6 us
    all_to_all x1, blocking collectives, body(): far = lax.all_to_all(line(gathered), ('x', 'y'), 0, 0, tiled=True)  18.9 us
    all_to_all x1, blocking collectives, body(): lax.all_to_all(step(place, strength, far), ('x', 'y'), 0, 0, tiled=True)  13.9 us
    pallas_call x5, Pallas kernels, call(): pl.pallas_call(kernel, out_shape=outs, in_specs=[spec() for _ in operands...  9.56 us
    all_gather x1, blocking collectives, body(): sides = lax.all_gather(side, 'c', axis=0, tiled=True)  6.65 us

profile of v1, /device:TPU:1, one launch (start us, length us, event | category | flops | bytes accessed | tf_op | source)
XLA Modules:
  0.0 78.7 jit_solution(7780020480066554679)
XLA Ops:
  0.6 0.0 copy-start.4
  0.6 0.0 copy-start.2
  0.7 0.0 copy-start.3
  0.7 0.6 copy-done.4
  1.3 0.0 copy-done.2
  1.3 0.0 copy-done.3
  1.3 0.0 copy-start
  1.3 0.7 copy-done
  2.0 0.1 shard_map.67
  2.1 27.6 %all_to_all.15.in_ref = bf16[16,16,128]{2,1,0:T(8,128)(2,1)S(1)} all-to-all(bf16[16,16,128]{2,1,0:T(8,128)(2,1)S(1)} %shard_map.67), channel_id=1, replica_groups=mesh['x'=4,'zl'=8,'y'=4,'zh'=2,'c'=2] {'zl','zh'}, dimensions={0} | all-to-all | bytes 131072 | tf_op jit(solution)/shard_map/all_to_all | solution.py:317
  29.8 0.2 shard_map.68
  30.0 18.9 %all_to_all.16.refs_0_ = bf16[16,208,128]{2,1,0:T(8,128)(2,1)S(1)} all-to-all(bf16[16,208,128]{2,1,0:T(8,128)(2,1)S(1)} %shard_map.68), channel_id=1, replica_groups=mesh['x'=4,'zl'=8,'y'=4,'zh'=2,'c'=2] {'x','y'}, dimensions={0} | all-to-all | bytes 1703936 | tf_op jit(solution)/shard_map/all_to_all | solution.py:318
  48.9 6.7 %shard_map.69 = bf16[16,208,128]{2,1,0:T(8,128)(2,1)S(1)} custom-call(bf16[16,208,128]{2,1,0:T(8,128)(2,1)S(1)} %all_to_all.16.refs_0_), custom_call_target="tpu_custom_call" | custom-call | tf_op jit(solution)/shard_map/pallas_call | solution.py:259
  55.6 0.0 copy-start.1
  55.6 13.9 %all_to_all.17.refs_1_ = bf16[16,208,128]{2,1,0:T(8,128)(2,1)S(1)} all-to-all(bf16[16,208,128]{2,1,0:T(8,128)(2,1)S(1)} %shard_map.69), channel_id=1, replica_groups=mesh['x'=4,'zl'=8,'y'=4,'zh'=2,'c'=2] {'x','y'}, dimensions={0} | all-to-all | bytes 1703936 | tf_op jit(solution)/shard_map/all_to_all | solution.py:319
  69.5 0.0 copy-done.1
  69.5 1.9 %shard_map.70 = (f32[3,16,32]{2,1,0:T(8,128)S(1)}, f32[8,128]{1,0:T(8,128)S(1)}) custom-call(bf16[16,208,128]{2,1,0:T(8,128)(2,1)S(1)} %all_to_all.16.refs_0_, bf16[16,208,128]{2,1,0:T(8,128)(2,1)S(1)} %all_to_all.17.refs_1_, f32[1,32]{1,0:T(1,128)S(1)} %bitcast.4, bf16[3,16,32]{2,1,0:T(8,128)(2,1)S(1)} %copy-done.1), custom_call_target="tpu_custom_call" | custom-call | tf_op jit(solution)/shard_map/pallas_call | solution.py:259
  71.4 6.7 %all_gather.3.refs_0_ = f32[16,128]{1,0:T(8,128)S(1)} all-gather(f32[8,128]{1,0:T(8,128)S(1)} %get-tuple-element.8), channel_id=1, replica_groups=mesh['x'=4,'zl'=8,'y'=4,'zh'=2,'c'=2] {'c'}, dimensions={0}, use_global_device_ids=true | all-gather | bytes 12288 | tf_op jit(solution)/shard_map/all_gather | solution.py:321
  78.1 0.6 shard_map.71
Async XLA Ops:
  0.6 0.7 copy-start.4
  0.6 0.7 copy-start.2
  0.7 0.7 copy-start.3
  1.3 0.7 copy-start
  55.6 13.9 %copy-start.1 = (bf16[3,16,32]{2,1,0:T(8,128)(2,1)S(1)}, bf16[3,16,32]{2,1,0:T(8,128)(2,1)}, u32[]{:S(2)}) copy-start(bf16[3,16,32]{2,1,0:T(8,128)(2,1)} %refs_3_.1) | copy-start | bytes 9220
